TPU v7x, 32 devices: a whole 2x2x4 slice. The times are simulated.
32 devices in a mesh: grp: 2 (over y), gx: 4 (over x, core), gy: 4 (over z).
Axes of the slice: x: 2, y: 2, z: 4, core: 2. Of those that a mesh axis runs over, the one named last changes fastest.
Arguments:
- tokens: bfloat16 [2048, 18432], P(('grp', 'gy'), 'gx'), parts along dimension 0, may hold values from -6 to 6
- gate_weight: bfloat16 [18432, 9216], P('gx', ('grp', 'gy')), parts along dimension 1, may hold values from -0.046875 to 0.046875
- up_weight: bfloat16 [18432, 9216], P('gx', ('grp', 'gy')), parts along dimension 1, may hold values from -0.046875 to 0.046875
- down_weight: bfloat16 [9216, 18432], P(('grp', 'gy'), 'gx'), parts along dimension 0, may hold values from -0.09375 to 0.09375
Outputs:
- mixed: bfloat16 [2048, 18432], P(('grp', 'gy'), 'gx'), parts along dimension 0
There are 2 independent parts, one for each index of `grp`. A program takes and returns all parts, laid end to end along the dimension named above; each array names one. Nothing has to cross between parts.
All inputs are finite; a program needn't handle non-finite values.
Results may differ from a plain program's by a relative error of at most 0.02.
Values may be sent and summed in bfloat16 or wider, within the bound.
A program may use at most 128 MiB of HBM per device.

v0:
```python
import jax
import jax.numpy as jnp
from jax import lax
from jax.sharding import PartitionSpec as P


def on_device(tokens, gate_weight, up_weight, down_weight):
    units_dev = gate_weight.shape[1]
    w_both = jnp.concatenate([gate_weight, up_weight], axis=1)
    gathered = lax.all_gather(tokens, "gy", axis=0, tiled=True)
    segment = gathered
    shares = lax.psum_scatter(
        jnp.dot(segment, w_both, preferred_element_type=jnp.float32).astype(jnp.bfloat16),
        "gx",
        scatter_dimension=0,
        tiled=True,
    ).astype(jnp.float32)
    gate_part = shares[:, :units_dev]
    up_part = shares[:, units_dev:]
    hidden = (jax.nn.silu(gate_part) * up_part).astype(jnp.bfloat16)
    hidden_all = lax.all_gather(hidden, "gx", axis=0, tiled=True)
    segment = hidden_all
    return lax.psum_scatter(
        jnp.dot(segment, down_weight, preferred_element_type=jnp.float32).astype(jnp.bfloat16),
        "gy",
        scatter_dimension=0,
        tiled=True,
    )


def solution(mesh):
    in_specs = (
        P(("grp", "gy"), "gx"),
        P("gx", ("grp", "gy")),
        P("gx", ("grp", "gy")),
        P(("grp", "gy"), "gx"),
    )
    out_specs = P(("grp", "gy"), "gx")
    return jax.shard_map(
        on_device, mesh=mesh, in_specs=in_specs, out_specs=out_specs, check_vma=False
    )
```

profile of v0, /device:TPU:0, one launch (start us, length us, event | category | flops | bytes accessed | tf_op | source)
XLA Modules:
  0.0 467.1 jit_solution(3209060373236941953)
XLA Ops:
  6.5 0.0 all-gather.3.cloned.1.call-start
  6.5 0.7 all-gather.3.cloned.1.call-update
  7.3 0.0 reduce-scatter.3.cloned.1.call-start
  7.3 171.1 %all-gather.3.cloned.1.call-done = bf16[1024,4608]{1,0:T(8,128)(2,1)} async-done(((bf16[256,4608]{1,0:T(8,128)(2,1)}), bf16[1024,4608]{1,0:T(8,128)(2,1)}) %all-gather.3.cloned.1.call-update) | async-done | bytes 9437200 | tf_op jit(solution)/shard_map/all_gather | solution.py:10
  178.4 29.1 %fusion.7 = bf16[1024,2304]{0,1:T(8,128)(2,1)} fusion(bf16[1024,4608]{1,0:T(8,128)(2,1)} %all-gather.3.cloned.1.call-done, bf16[4608,1152]{1,0:T(8,128)(2,1)} %param.6, bf16[4608,1152]{1,0:T(8,128)(2,1)} %param.5), kind=kOutput, calls=%fused_computation.6 | convolution fusion | flops 21788098560 | bytes 35389440 | tf_op jit(solution)/shard_map/dot_general | solution.py:13
  207.6 0.0 reduce-scatter.3.cloned.1.call-update
  207.6 0.0 all-gather.5.cloned.1.call-start
  207.6 46.1 %reduce-scatter.3.cloned.1.call-done = bf16[256,2304]{0,1:T(8,128)(2,1)} async-done(((bf16[1024,2304]{0,1:T(8,128)(2,1)}), bf16[256,2304]{0,1:T(8,128)(2,1)}) %reduce-scatter.3.cloned.1.call-update) | async-done | bytes 1179664 | tf_op jit(solution)/shard_map/reduce_scatter | solution.py:12
  253.8 1.4 convert_element_type.17
  255.2 1.2 fusion.10
  256.4 0.0 all-gather.5.cloned.1.call-update
  256.4 0.2 reduce-scatter.5.cloned.1.call-start
  256.7 24.3 %all-gather.5.cloned.1.call-done = bf16[1024,1152]{0,1:T(8,128)(2,1)} async-done(((bf16[256,1152]{0,1:T(8,128)(2,1)}), bf16[1024,1152]{0,1:T(8,128)(2,1)}) %all-gather.5.cloned.1.call-update) | async-done | bytes 2359312 | tf_op jit(solution)/shard_map/all_gather | solution.py:21
  280.9 18.2 %convolution_convert_fusion = bf16[1024,4608]{1,0:T(8,128)(2,1)} fusion(bf16[1024,1152]{0,1:T(8,128)(2,1)} %all-gather.5.cloned.1.call-done, bf16[1152,4608]{1,0:T(8,128)(2,1)} %param.7), kind=kOutput, calls=%fused_computation.4 | convolution fusion | flops 10876354560 | bytes 22413312 | tf_op jit(solution)/shard_map/dot_general | solution.py:24
  299.2 0.0 reduce-scatter.5.cloned.1.call-update
  299.2 161.4 %reduce-scatter.5.cloned.1.call-done = bf16[256,4608]{1,0:T(8,128)(2,1)} async-done(((bf16[1024,4608]{1,0:T(8,128)(2,1)}), bf16[256,4608]{1,0:T(8,128)(2,1)}) %reduce-scatter.5.cloned.1.call-update) | async-done | bytes 2359312 | tf_op jit(solution)/shard_map/reduce_scatter | solution.py:23
Async XLA Ops:
  6.5 171.9 %all-gather.3.cloned.1.call-start = ((), (), s32[]{:S(2)}) async-start(), calls=%async_computation.2 | async-start | bytes 11796480 | tf_op jit(solution)/shard_map/all_gather | solution.py:10
  7.3 246.5 %reduce-scatter.3.cloned.1.call-start = ((), (), s32[]{:S(2)}) async-start(), calls=%async_computation.3 | async-start | bytes 5898240 | tf_op jit(solution)/shard_map/reduce_scatter | solution.py:12
  207.6 73.4 %all-gather.5.cloned.1.call-start = ((), (), s32[]{:S(2)}) async-start(), calls=%async_computation.4 | async-start | bytes 2949120 | tf_op jit(solution)/shard_map/all_gather | solution.py:21
  256.4 204.2 %reduce-scatter.5.cloned.1.call-start = ((), (), s32[]{:S(2)}) async-start(), calls=%async_computation.5 | async-start | bytes 11796480 | tf_op jit(solution)/shard_map/reduce_scatter | solution.py:23
Sparse Core Ops, SparseCore 0:
  8.9 169.4 all-gather.2
  207.7 46.0 reduce-scatter.2
  256.5 24.3 all-gather.4
  299.3 161.2 reduce-scatter.4
where the time goes:
time: 467 us
  waiting for transfers between devices  404 us (87%)
  matrix products  47.3 us (10%)
  between operations  13.1 us (3%)
    all_gather x1, waiting for transfers between devices, on_device(): gathered = lax.all_gather(tokens, 'gy', axis=0, tiled=True)  171 us
    reduce_scatter x1, waiting for transfers between devices, on_device(): lax.psum_scatter(jnp.dot(segment, down_weight, preferred_element_type=jnp...  161 us
    reduce_scatter x1, waiting for transfers between devices, on_device(): lax.psum_scatter(jnp.dot(segment, w_both, preferred_element_type=jnp.floa...  46.1 us
    dot_general x1, matrix products, on_device(): jnp.dot(segment, w_both, preferred_element_type=jnp.float32)  29.1 us
    all_gather x1, waiting for transfers between devices, on_device(): hidden_all = lax.all_gather(hidden, 'gx', axis=0, tiled=True)  24.3 us
    dot_general x1, matrix products, on_device(): jnp.dot(segment, down_weight, preferred_element_type=jnp.float32)  18.2 us
  transfers between devices with their start and end apart: 4, of which 4 were waited for; matrix products, arithmetic and copies ran while one was open for 0% of the time, Pallas kernels for 0%

commit v1 on v0

v1 whole, which is shorter than its diff:
```python
import functools

import jax
import jax.numpy as jnp
from jax import lax
from jax.experimental import pallas as pl
from jax.experimental.pallas import tpu as pltpu
from jax.sharding import PartitionSpec as P

MESH = pl.DeviceIdType.MESH
CHUNKS = 8
TILE = 256
F32 = jnp.float32
BF16 = jnp.bfloat16


def fused(
    n_gx, n_gy, chunks,
    tok, wg, wu, wd, out,
    w_in, w_down, xg, sums, gu, gu_in, hid,
    w_sem, own_sem, out_sem,
    ag_send, ag_recv, rs_send, rs_recv, gu_send, gu_recv, h_send, h_recv,
):
    x = lax.axis_index("gx")
    z = lax.axis_index("gy")
    last = n_gy - 1
    rows = xg.shape[2]
    width = xg.shape[3]
    units = hid.shape[2]
    part = hid.shape[1]
    total = n_gy * rows

    def peer(o):
        return lax.rem(x + o, n_gx)

    barrier = pltpu.get_barrier_semaphore()
    for o in range(1, n_gx):
        pl.semaphore_signal(barrier, inc=1, device_id={"gx": peer(o)}, device_id_type=MESH)

    @pl.when(z > 0)
    def _():
        pl.semaphore_signal(barrier, inc=1, device_id={"gy": z - 1}, device_id_type=MESH)

    @pl.when(z < last)
    def _():
        pl.semaphore_signal(barrier, inc=1, device_id={"gy": z + 1}, device_id_type=MESH)

    def own_copy(c):
        return pltpu.make_async_copy(tok.at[pl.ds(c * rows, rows)], xg.at[c, z], own_sem.at[c])

    loads = [
        pltpu.make_async_copy(wg, w_in.at[:, pl.ds(0, units)], w_sem.at[0]),
        pltpu.make_async_copy(wu, w_in.at[:, pl.ds(units, units)], w_sem.at[1]),
        pltpu.make_async_copy(wd, w_down, w_sem.at[2]),
    ]

    pl.semaphore_wait(barrier, n_gx - 1 + jnp.where(z > 0, 1, 0) + jnp.where(z < last, 1, 0))

    def ag_copy(c, q, to, own):
        q_sem = jnp.where(to < z, n_gy, q) if own else q
        src = tok.at[pl.ds(c * rows, rows)] if own else xg.at[c, q]
        return pltpu.make_async_remote_copy(
            src_ref=src, dst_ref=xg.at[c, q],
            send_sem=ag_send.at[c, q_sem], recv_sem=ag_recv.at[c, q],
            device_id={"gy": to}, device_id_type=MESH,
        )

    def ag_first(c):
        @pl.when(z < last)
        def _():
            ag_copy(c, z, z + 1, True).start()

        @pl.when(z > 0)
        def _():
            ag_copy(c, z, z - 1, True).start()

    def ag_step(c, s):
        @pl.when(z - s >= 0)
        def _():
            q = z - s
            ag_copy(c, q, z - 1, False).wait_recv()

            @pl.when(z < last)
            def _():
                ag_copy(c, q, z + 1, False).start()

        @pl.when(z + s <= last)
        def _():
            q = z + s
            ag_copy(c, q, z + 1, False).wait_recv()

            @pl.when(z > 0)
            def _():
                ag_copy(c, q, z - 1, False).start()

    def ag_sent(c):
        @pl.when(z < last)
        def _():
            ag_copy(c, z, z + 1, True).wait_send()

        @pl.when(z > 0)
        def _():
            ag_copy(c, z, z - 1, True).wait_send()

        for s in range(1, n_gy):
            @pl.when((z - s >= 0) & (z < last))
            def _():
                ag_copy(c, z - s, z + 1, False).wait_send()

            @pl.when((z + s <= last) & (z > 0))
            def _():
                ag_copy(c, z + s, z - 1, False).wait_send()

    def gu_copy(o):
        return pltpu.make_async_remote_copy(
            src_ref=gu.at[peer(o)], dst_ref=gu_in.at[o - 1],
            send_sem=gu_send.at[o - 1], recv_sem=gu_recv.at[o - 1],
            device_id={"gx": peer(o)}, device_id_type=MESH,
        )

    def h_copy(o):
        return pltpu.make_async_remote_copy(
            src_ref=hid.at[x], dst_ref=hid.at[x],
            send_sem=h_send.at[o - 1], recv_sem=h_recv.at[o - 1],
            device_id={"gx": peer(o)}, device_id_type=MESH,
        )

    def gate_up(c):
        own_copy(c).wait()

        @pl.when(c == 0)
        def _():
            loads[0].wait()
            loads[1].wait()

        @pl.loop(0, 2 * units // TILE)
        def _(i):
            cols = pl.ds(pl.multiple_of(i * TILE, TILE), TILE)
            prod = jnp.dot(
                xg[c].reshape(total, width), w_in[:, cols], preferred_element_type=F32
            )
            gu[:, :, cols] = prod.astype(BF16).reshape(n_gx, part, TILE)

        for o in range(1, n_gx):
            gu_copy(o).start()

    def hidden(c):
        for o in range(1, n_gx):
            gu_copy(o).wait_recv()

        @pl.loop(0, units // 128)
        def _(i):
            a = pl.ds(pl.multiple_of(i * 128, 128), 128)
            b = pl.ds(pl.multiple_of(units + i * 128, 128), 128)
            gate = gu[x, :, a].astype(F32)
            up = gu[x, :, b].astype(F32)
            for o in range(n_gx - 1):
                gate += gu_in[o, :, a].astype(F32)
                up += gu_in[o, :, b].astype(F32)
            hid[x, :, a] = (gate / (1.0 + jnp.exp(-gate)) * up).astype(BF16)

        for o in range(1, n_gx):
            h_copy(o).start()
        for o in range(1, n_gx):
            gu_copy(o).wait_send()

    def down(c):
        @pl.when(c == 0)
        def _():
            loads[2].wait()

        ag_sent(c)
        for o in range(1, n_gx):
            h_copy(o).wait_recv()

        @pl.loop(0, width // TILE)
        def _(i):
            cols = pl.ds(pl.multiple_of(i * TILE, TILE), TILE)
            prod = jnp.dot(
                hid[...].reshape(total, units), w_down[:, cols], preferred_element_type=F32
            )
            xg[c, :, :, cols] = prod.astype(BF16).reshape(n_gy, rows, TILE)

        for o in range(1, n_gx):
            h_copy(o).wait_send()

    def rs_copy(c, d, to):
        slot = jnp.where((to < z) & (d == to), n_gy, d)
        return pltpu.make_async_remote_copy(
            src_ref=xg.at[c, d], dst_ref=sums.at[c, slot],
            send_sem=rs_send.at[c, d], recv_sem=rs_recv.at[c, slot],
            device_id={"gy": to}, device_id_type=MESH,
        )

    def rs_arrived(c, slot, frm):
        pltpu.make_async_remote_copy(
            src_ref=xg.at[c, 0], dst_ref=sums.at[c, slot],
            send_sem=rs_send.at[c, 0], recv_sem=rs_recv.at[c, slot],
            device_id={"gy": frm}, device_id_type=MESH,
        ).wait_recv()

    def add(c, d, slots):
        step = 512 if width % 512 == 0 else 128

        @pl.loop(0, width // step)
        def _(i):
            cols = pl.ds(pl.multiple_of(i * step, step), step)
            acc = xg[c, d, :, cols].astype(F32)
            for slot in slots:
                acc += sums[c, slot, :, cols].astype(F32)
            xg[c, d, :, cols] = acc.astype(BF16)

    def rs_step(c, t):
        @pl.when((z <= t) & (z < last))
        def _():
            d = last - (t - z)

            @pl.when(z > 0)
            def _():
                rs_arrived(c, d, z - 1)
                add(c, d, [d])

            rs_copy(c, d, z + 1).start()

        @pl.when((last - z <= t) & (z > 0))
        def _():
            d = t - (last - z)

            @pl.when(z < last)
            def _():
                rs_arrived(c, d, z + 1)
                add(c, d, [d])

            rs_copy(c, d, z - 1).start()

    def out_copy(c):
        return pltpu.make_async_copy(xg.at[c, z], out.at[pl.ds(c * rows, rows)], out_sem.at[c])

    def rs_last(c):
        @pl.when(z > 0)
        def _():
            rs_arrived(c, z, z - 1)

        @pl.when(z < last)
        def _():
            rs_arrived(c, n_gy, z + 1)

        @pl.when((z > 0) & (z < last))
        def _():
            add(c, z, [z, n_gy])

        @pl.when(z == 0)
        def _():
            add(c, z, [n_gy])

        @pl.when(z == last)
        def _():
            add(c, z, [z])

        out_copy(c).start()

    def finish(c):
        out_copy(c).wait()
        for d in range(n_gy):
            @pl.when(d > z)
            def _():
                rs_copy(c, d, z + 1).wait_send()

            @pl.when(d < z)
            def _():
                rs_copy(c, d, z - 1).wait_send()

    ag_first(0)
    own_copy(0).start()
    for load in loads:
        load.start()
    for c in range(1, chunks):
        own_copy(c).start()

    @pl.loop(0, chunks + 2)
    def _(p):
        def when(c, f, *args):
            @pl.when((c >= 0) & (c < chunks))
            def _():
                f(c, *args)

        when(p - 1, gate_up)
        when(p, ag_step, 1)
        when(p - 2, rs_step, 1)
        when(p - 1, hidden)
        for s in range(2, last):
            when(p, ag_step, s)
            if s == 2:
                when(p + 1, ag_first)
            when(p - 2, rs_step, s)
        when(p - 1, down)
        when(p - 1, rs_step, 0)
        when(p, ag_step, last)
        when(p - 2, rs_last)

    @pl.loop(0, chunks)
    def _(c):
        finish(c)


def on_device_fused(n_gx, n_gy, tokens, gate_weight, up_weight, down_weight):
    held, width = tokens.shape
    units = gate_weight.shape[1]
    chunks = CHUNKS
    rows = held // chunks
    part = n_gy * rows // n_gx
    dma = pltpu.SemaphoreType.DMA
    return pl.pallas_call(
        functools.partial(fused, n_gx, n_gy, chunks),
        out_shape=jax.ShapeDtypeStruct((held, width), BF16),
        in_specs=[pl.BlockSpec(memory_space=pl.ANY)] * 4,
        out_specs=pl.BlockSpec(memory_space=pl.ANY),
        scratch_shapes=[
            pltpu.VMEM((width, 2 * units), BF16),
            pltpu.VMEM((units, width), BF16),
            pltpu.VMEM((chunks, n_gy, rows, width), BF16),
            pltpu.VMEM((chunks, n_gy + 1, rows, width), BF16),
            pltpu.VMEM((n_gx, part, 2 * units), BF16),
            pltpu.VMEM((n_gx - 1, part, 2 * units), BF16),
            pltpu.VMEM((n_gx, part, units), BF16),
            dma((3,)),
            dma((chunks,)),
            dma((chunks,)),
            dma((chunks, n_gy + 1)),
            dma((chunks, n_gy)),
            dma((chunks, n_gy)),
            dma((chunks, n_gy + 1)),
            dma((n_gx - 1,)),
            dma((n_gx - 1,)),
            dma((n_gx - 1,)),
            dma((n_gx - 1,)),
        ],
        compiler_params=pltpu.CompilerParams(
            collective_id=0, has_side_effects=True, vmem_limit_bytes=62 * 1024 * 1024
        ),
        cost_estimate=pl.CostEstimate(
            flops=6 * n_gy * held * width * units,
            bytes_accessed=2 * (3 * width * units + 2 * held * width),
            transcendentals=n_gy * held * units // n_gx,
        ),
    )(tokens, gate_weight, up_weight, down_weight)


def on_device_plain(tokens, gate_weight, up_weight, down_weight):
    units_dev = gate_weight.shape[1]
    w_both = jnp.concatenate([gate_weight, up_weight], axis=1)
    gathered = lax.all_gather(tokens, "gy", axis=0, tiled=True)
    shares = lax.psum_scatter(
        jnp.dot(gathered, w_both, preferred_element_type=F32).astype(BF16),
        "gx",
        scatter_dimension=0,
        tiled=True,
    ).astype(F32)
    hidden = (jax.nn.silu(shares[:, :units_dev]) * shares[:, units_dev:]).astype(BF16)
    hidden_all = lax.all_gather(hidden, "gx", axis=0, tiled=True)
    return lax.psum_scatter(
        jnp.dot(hidden_all, down_weight, preferred_element_type=F32).astype(BF16),
        "gy",
        scatter_dimension=0,
        tiled=True,
    )


def solution(mesh):
    n_gx, n_gy = mesh.shape["gx"], mesh.shape["gy"]
    in_specs = (
        P(("grp", "gy"), "gx"),
        P("gx", ("grp", "gy")),
        P("gx", ("grp", "gy")),
        P(("grp", "gy"), "gx"),
    )

    def on_device(tokens, gate_weight, up_weight, down_weight):
        held, width = tokens.shape
        units = gate_weight.shape[1]
        rows = held // CHUNKS
        fits = (
            held % (16 * CHUNKS) == 0
            and n_gy * rows % (16 * n_gx) == 0
            and units % 128 == 0
            and width % TILE == 0
            and n_gx > 1
            and n_gy > 3
        )
        if fits:
            return on_device_fused(n_gx, n_gy, tokens, gate_weight, up_weight, down_weight)
        return on_device_plain(tokens, gate_weight, up_weight, down_weight)

    return jax.shard_map(
        on_device,
        mesh=mesh,
        in_specs=in_specs,
        out_specs=P(("grp", "gy"), "gx"),
        check_vma=False,
    )
```

time: 467 us -> 280 us (0.60)
  waiting for transfers between devices: 404 us -> 0 us
  Pallas kernels: 0 us -> 276 us
  matrix products: 47.3 us -> 0 us
  between operations: 13.1 us -> 0.01 us
    pallas_call x0 -> x1, Pallas kernels: none -> 276 us  [on_device_fused(): pl.pallas_call(functools.partial(fused, n_gx, n_gy, chunks), out_shape=ja...]
    reduce_scatter x2 -> x0, waiting for transfers between devices: 208 us -> none  [the longest x1 161 us: on_device(): lax.psum_scatter(jnp.dot(segment, down_weight, preferred_element_type=jnp...]
    all_gather x2 -> x0, waiting for transfers between devices: 195 us -> none  [the longest x1 171 us: on_device(): gathered = lax.all_gather(tokens, 'gy', axis=0, tiled=True)]
    dot_general x2 -> x0, matrix products: 47.3 us -> none  [the longest x1 29.1 us: on_device(): jnp.dot(segment, w_both, preferred_element_type=jnp.float32)]
  transfers between devices with their start and end apart: 4 -> 0, of which waited for: 4 -> 0; matrix products, arithmetic and copies ran while one was open for 0% -> 0% of each run, Pallas kernels for 0% -> 0%
where the time goes in v1:
time: 280 us; the launch traced here: 279 us
  Pallas kernels  276 us (99%)
  local copies, waits for them, and re-layouts  3.22 us (1%)
    pallas_call x1, Pallas kernels, on_device_fused(): pl.pallas_call(functools.partial(fused, n_gx, n_gy, chunks), out_shape=ja...  276 us

profile of v1, /device:TPU:0, one launch (start us, length us, event | category | flops | bytes accessed | tf_op | source)
XLA Modules:
  0.0 279.5 jit_solution(2653092913510289591)
XLA Ops:
  0.0 276.2 %shard_map.46 = bf16[256,4608]{1,0:T(8,128)(2,1)} custom-call(bf16[256,4608]{1,0:T(8,128)(2,1)} %tok.1, bf16[4608,1152]{1,0:T(8,128)(2,1)} %wg.1, bf16[4608,1152]{1,0:T(8,128)(2,1)} %wu.1, bf16[1152,4608]{1,0:T(8,128)(2,1)} %wd.1), custom_call_target="tpu_custom_call" | custom-call | flops 32614907904 | bytes 36569088 | tf_op jit(solution)/shard_map/pallas_call | solution.py:313
  276.2 3.2 %copy.6 = bf16[256,4608]{1,0:T(8,128)(2,1)} copy(bf16[256,4608]{1,0:T(8,128)(2,1)} %shard_map.46) | data formatting | bytes 4718592

commit v2 on v1

--- a/solution.py
+++ b/solution.py
@@ -9,7 +9,7 @@
 
 MESH = pl.DeviceIdType.MESH
 CHUNKS = 8
-TILE = 256
+TILE = 768
 F32 = jnp.float32
 BF16 = jnp.bfloat16
 
@@ -284,18 +284,16 @@
             def _():
                 f(c, *args)
 
+        when(p, ag_step, 1)
+        when(p + 1, ag_first)
         when(p - 1, gate_up)
-        when(p, ag_step, 1)
         when(p - 2, rs_step, 1)
+        when(p, ag_step, 2)
         when(p - 1, hidden)
-        for s in range(2, last):
-            when(p, ag_step, s)
-            if s == 2:
-                when(p + 1, ag_first)
-            when(p - 2, rs_step, s)
+        when(p - 2, rs_step, 2)
+        when(p, ag_step, 3)
         when(p - 1, down)
         when(p - 1, rs_step, 0)
-        when(p, ag_step, last)
         when(p - 2, rs_last)
 
     @pl.loop(0, chunks)

time: 280 us -> 257 us (0.918)
  Pallas kernels: 276 us -> 254 us
    pallas_call x1, Pallas kernels: 276 us -> 254 us  [on_device_fused(): pl.pallas_call(functools.partial(fused, n_gx, n_gy, chunks), out_shape=ja...]
where the time goes in v2:
time: 257 us
  Pallas kernels  254 us (99%)
  local copies, waits for them, and re-layouts  3.22 us (1%)
    pallas_call x1, Pallas kernels, on_device_fused(): pl.pallas_call(functools.partial(fused, n_gx, n_gy, chunks), out_shape=ja...  254 us

profile of v2, /device:TPU:0, one launch (start us, length us, event | category | flops | bytes accessed | tf_op | source)
XLA Modules:
  0.0 257.3 jit_solution(4672629647584549279)
XLA Ops:
  0.0 254.1 %shard_map.46 = bf16[256,4608]{1,0:T(8,128)(2,1)} custom-call(bf16[256,4608]{1,0:T(8,128)(2,1)} %tok.1, bf16[4608,1152]{1,0:T(8,128)(2,1)} %wg.1, bf16[4608,1152]{1,0:T(8,128)(2,1)} %wu.1, bf16[1152,4608]{1,0:T(8,128)(2,1)} %wd.1), custom_call_target="tpu_custom_call" | custom-call | flops 32614907904 | bytes 36569088 | tf_op jit(solution)/shard_map/pallas_call | solution.py:311
  254.1 3.2 %copy.6 = bf16[256,4608]{1,0:T(8,128)(2,1)} copy(bf16[256,4608]{1,0:T(8,128)(2,1)} %shard_map.46) | data formatting | bytes 4718592

commit v3 on v2

--- a/solution.py
+++ b/solution.py
@@ -9,7 +9,7 @@
 
 MESH = pl.DeviceIdType.MESH
 CHUNKS = 8
-TILE = 768
+TILE = 1152
 F32 = jnp.float32
 BF16 = jnp.bfloat16
 
@@ -382,6 +382,7 @@
             and n_gy * rows % (16 * n_gx) == 0
             and units % 128 == 0
             and width % TILE == 0
+            and 2 * units % TILE == 0
             and n_gx > 1
             and n_gy > 3
         )

time: 257 us -> 257 us (level)
  no operation moved by 1% of the time
where the time goes in v3:
time: 257 us
  Pallas kernels  254 us (99%)
  local copies, waits for them, and re-layouts  3.22 us (1%)
    pallas_call x1, Pallas kernels, on_device_fused(): pl.pallas_call(functools.partial(fused, n_gx, n_gy, chunks), out_shape=ja...  254 us

profile of v3, /device:TPU:0, one launch (start us, length us, event | category | flops | bytes accessed | tf_op | source)
XLA Modules:
  0.0 257.1 jit_solution(4549321267367804856)
XLA Ops:
  0.0 253.9 %shard_map.46 = bf16[256,4608]{1,0:T(8,128)(2,1)} custom-call(bf16[256,4608]{1,0:T(8,128)(2,1)} %tok.1, bf16[4608,1152]{1,0:T(8,128)(2,1)} %wg.1, bf16[4608,1152]{1,0:T(8,128)(2,1)} %wu.1, bf16[1152,4608]{1,0:T(8,128)(2,1)} %wd.1), custom_call_target="tpu_custom_call" | custom-call | flops 32614907904 | bytes 36569088 | tf_op jit(solution)/shard_map/pallas_call | solution.py:311
  253.9 3.2 %copy.6 = bf16[256,4608]{1,0:T(8,128)(2,1)} copy(bf16[256,4608]{1,0:T(8,128)(2,1)} %shard_map.46) | data formatting | bytes 4718592
